TPU v7x, 512 devices: a whole 4x4x16 slice. The times are simulated.
512 devices in a mesh: dp: 64 (over y, z_lo, core), blk: 8 (over z_hi, x).
Axes of the slice: x: 4, y: 4, z: 16 (z_hi: 2, z_lo: 8; z = z_hi * 8 + z_lo), core: 2. Of those that a mesh axis runs over, the one named last changes fastest.
Arguments:
- images: float32 [65536, 1152], P(('dp', 'blk')), may hold values from -12 to 12
- texts: float32 [65536, 1152], P(('dp', 'blk')), may hold values from -6 to 6
- positives: int32 [65536], P(('dp', 'blk')), may hold values from 0 to 127, as said below
- plan: int32 [3, 64], replicated, may hold values from 0 to 63, as said below
Outputs:
- image_grad: float32 [65536, 1152], P(('dp', 'blk'))
- text_grad: float32 [65536, 1152], P(('dp', 'blk'))
- totals: float32 [3], replicated
Inputs may be any that keep to these rules, and one draw needn't show every extreme that they name: Within each device's block of 128 rows, positives holds every number 0 to 127 once. Each row of plan pairs the indices of dp: plan[r, plan[r, a]] = a and plan[r, a] != a. No two rounds pair the same two indices.
All inputs are finite; a program needn't handle non-finite values.
Results may differ from a plain program's by a relative error of at most 0.005.
Values may be sent and summed in bfloat16 or wider, within the bound.
A program may use at most 64 MiB of HBM per device.

v0:
```python
import math

import jax
import jax.numpy as jnp
from jax import lax
from jax.sharding import PartitionSpec as P

LOGIT_SHARPNESS = 2.0
LOGIT_OFFSET = -2.0


def similarity(left, right, scale_factor):
    return (
        lax.dot_general(left, right, (((1,), (1,)), ((), ())), preferred_element_type=jnp.float32)
        * scale_factor
    )


def pair_terms(similarity_matrix, target_signs):
    pair_logits = LOGIT_SHARPNESS * similarity_matrix + LOGIT_OFFSET
    weights = jax.nn.sigmoid(pair_logits) - target_signs
    losses = jax.nn.softplus(pair_logits) - target_signs * pair_logits
    stats = jnp.stack([jnp.sum(losses), jnp.sum(weights), jnp.sum(weights * similarity_matrix)])
    return (weights.astype(jnp.bfloat16), stats)


def row_sum(weights, other):
    return jnp.dot(weights, other, preferred_element_type=jnp.float32)


def column_sum(weights, other):
    return lax.dot_general(
        weights, other, (((0,), (0,)), ((), ())), preferred_element_type=jnp.float32
    )


def body(images, texts, positives, plan):
    rows, width = images.shape
    peers = lax.axis_size("dp")
    share = rows // peers
    rounds = plan.shape[0]
    scale_factor = 1.0 / math.sqrt(width)
    gradient_factor = LOGIT_SHARPNESS * scale_factor
    left = images.astype(jnp.bfloat16)
    right = texts.astype(jnp.bfloat16)
    target_signs = (jnp.arange(rows, dtype=jnp.int32)[None, :] == positives[:, None]).astype(
        jnp.float32
    )
    weights, stats = pair_terms(similarity(left, right, scale_factor), target_signs)
    image_acc = row_sum(weights, right)
    text_gradient_total = column_sum(weights, left)
    packed = right[None]
    count = packed.shape[0]
    arrived = []
    for step in range(rounds):
        spread_one = lax.all_to_all(packed, "dp", split_axis=1, concat_axis=1, tiled=True)
        reorder_slots = spread_one.reshape(count, peers, share, width)
        arrived.append(
            lax.all_to_all(
                jnp.take(reorder_slots, plan[step], axis=1).reshape(count, rows, width),
                "dp",
                split_axis=1,
                concat_axis=1,
                tiled=True,
            )
        )
    returned = []
    for step in range(rounds):
        their_right = arrived[step][count - 1]
        forward, extra = pair_terms(similarity(left, their_right, scale_factor), 0.0)
        stats = stats + extra
        image_acc = image_acc + row_sum(forward, their_right)
        returned.append(column_sum(forward, left) * gradient_factor)
    text_grad = text_gradient_total * gradient_factor
    spread_back = lax.all_to_all(jnp.stack(returned), "dp", split_axis=1, concat_axis=1, tiled=True)
    slots = spread_back.reshape(rounds, peers, share, width)
    summed = jnp.take(slots[0], plan[0], axis=0)
    for step in range(1, rounds):
        summed = summed + jnp.take(slots[step], plan[step], axis=0)
    text_grad = text_grad + lax.all_to_all(
        summed.reshape(rows, width), "dp", split_axis=0, concat_axis=0, tiled=True
    )
    pairs = float(rows * rows * (rounds + 1) * peers * lax.axis_size("blk"))
    totals = lax.psum(stats, ("dp", "blk")) / pairs
    return (image_acc * gradient_factor, text_grad, totals)


def solution(mesh):
    placed = (P(("dp", "blk"), None), P(("dp", "blk"), None), P(("dp", "blk")), P())
    return jax.shard_map(
        body,
        mesh=mesh,
        in_specs=placed,
        out_specs=(P(("dp", "blk"), None), P(("dp", "blk"), None), P()),
        check_vma=False,
    )
```

profile of v0, /device:TPU:1, one launch (start us, length us, event | category | flops | bytes accessed | tf_op | source)
XLA Modules:
  0.0 391.3 jit_solution(8783394955422144393)
XLA Ops:
  0.6 1.1 convert_bitcast_fusion
  1.7 0.5 copy.84
  2.2 0.5 broadcast.174
  2.7 2.4 reduce.8
  5.1 0.8 reshape.142
  6.0 17.2 %all-to-all-start = ((bf16[64,2,1152]{2,1,0:T(2,128)(2,1)}), bf16[64,2,1152]{2,1,0:T(2,128)(2,1)S(1)}, u32[]{:S(2)}, u32[]{:S(2)}) async-start(bf16[64,2,1152]{2,1,0:T(2,128)(2,1)} %reshape.142), calls=%async_computation | async-start | bytes 589824 | tf_op jit(solution)/shard_map/all_to_all | solution.py:56
  23.2 20.5 %all-to-all-done = bf16[64,2,1152]{2,1,0:T(2,128)(2,1)S(1)} async-done(((bf16[64,2,1152]{2,1,0:T(2,128)(2,1)}), bf16[64,2,1152]{2,1,0:T(2,128)(2,1)S(1)}, u32[]{:S(2)}, u32[]{:S(2)}) %all-to-all-start) | async-done | bytes 294944 | tf_op jit(solution)/shard_map/all_to_all | solution.py:56
  43.7 0.2 reshape.143
  44.0 1.7 bitcast_reduce_fusion
  45.6 0.1 reshape.114
  45.8 1.2 gather_fusion
  47.0 0.3 broadcast_select_fusion.2
  47.3 0.3 reshape.133
  47.6 2.4 reduce.9
  50.0 0.8 reshape.144
  50.8 7.0 %all-to-all-start.1 = ((bf16[64,2,1152]{2,1,0:T(2,128)(2,1)}), bf16[64,2,1152]{2,1,0:T(2,128)(2,1)S(1)}, u32[]{:S(2)}, u32[]{:S(2)}) async-start(bf16[64,2,1152]{2,1,0:T(2,128)(2,1)} %reshape.144), calls=%async_computation.1 | async-start | bytes 589824 | tf_op jit(solution)/shard_map/all_to_all | solution.py:59
  57.8 1.2 gather_fusion.2
  59.0 1.2 gather_fusion.1
  60.2 0.6 broadcast_select_fusion
  60.9 0.3 reshape.135
  61.1 2.4 reduce.10
  63.6 0.8 reshape.146
  64.4 14.0 %all-to-all-done.1 = bf16[64,2,1152]{2,1,0:T(2,128)(2,1)S(1)} async-done(((bf16[64,2,1152]{2,1,0:T(2,128)(2,1)}), bf16[64,2,1152]{2,1,0:T(2,128)(2,1)S(1)}, u32[]{:S(2)}, u32[]{:S(2)}) %all-to-all-start.1) | async-done | bytes 294944 | tf_op jit(solution)/shard_map/all_to_all | solution.py:59
  78.4 7.0 %all-to-all-start.2 = ((bf16[64,2,1152]{2,1,0:T(2,128)(2,1)}), bf16[64,2,1152]{2,1,0:T(2,128)(2,1)S(1)}, u32[]{:S(2)}, u32[]{:S(2)}) async-start(bf16[64,2,1152]{2,1,0:T(2,128)(2,1)} %reshape.146), calls=%async_computation.2 | async-start | bytes 589824 | tf_op jit(solution)/shard_map/all_to_all | solution.py:59
  85.3 0.3 reshape.137
  85.6 2.4 reduce.11
  88.0 0.8 reshape.148
  88.8 17.0 %all-to-all-done.2 = bf16[64,2,1152]{2,1,0:T(2,128)(2,1)S(1)} async-done(((bf16[64,2,1152]{2,1,0:T(2,128)(2,1)}), bf16[64,2,1152]{2,1,0:T(2,128)(2,1)S(1)}, u32[]{:S(2)}, u32[]{:S(2)}) %all-to-all-start.2) | async-done | bytes 294944 | tf_op jit(solution)/shard_map/all_to_all | solution.py:59
  105.9 7.0 %all-to-all-start.3 = ((bf16[64,2,1152]{2,1,0:T(2,128)(2,1)}), bf16[64,2,1152]{2,1,0:T(2,128)(2,1)S(1)}, u32[]{:S(2)}, u32[]{:S(2)}) async-start(bf16[64,2,1152]{2,1,0:T(2,128)(2,1)} %reshape.148), calls=%async_computation.3 | async-start | bytes 589824 | tf_op jit(solution)/shard_map/all_to_all | solution.py:59
  112.9 0.3 reshape.145
  113.2 0.3 reshape.147
  113.5 1.0 fusion.23
  114.5 0.9 fusion.25
  115.4 18.0 %all-to-all-done.3 = bf16[64,2,1152]{2,1,0:T(2,128)(2,1)S(1)} async-done(((bf16[64,2,1152]{2,1,0:T(2,128)(2,1)}), bf16[64,2,1152]{2,1,0:T(2,128)(2,1)S(1)}, u32[]{:S(2)}, u32[]{:S(2)}) %all-to-all-start.3) | async-done | bytes 294944 | tf_op jit(solution)/shard_map/all_to_all | solution.py:59
  133.4 0.2 reshape.149
  133.7 1.0 fusion.27
  134.7 0.3 fusion.4
  135.0 0.3 fusion.3
  135.3 0.3 fusion.2
  135.6 0.1 pad_maximum_fusion
  135.7 1.2 copy.38
  136.9 115.6 %all_to_all.36 = f32[3,128,1152]{2,0,1:T(4,128)S(1)} all-to-all(f32[3,128,1152]{2,0,1:T(4,128)S(1)} %copy.38), channel_id=1, replica_groups=mesh['dp'=64,'blk'=8] {'dp'}, dimensions={1} | all-to-all | bytes 3538944 | tf_op jit(solution)/shard_map/all_to_all | solution.py:75
  252.4 4.6 %slice_reduce_fusion.2 = (f32[128,1152]{1,0:T(8,128)S(1)}, f32[128,1152]{1,0:T(8,128)S(1)}, f32[128,1152]{1,0:T(8,128)S(1)}) fusion(f32[3,128,1152]{2,0,1:T(4,128)S(1)} %all_to_all.36), kind=kLoop, calls=%fused_computation.21 | loop fusion | bytes 3538944 | tf_op jit(solution)/shard_map/slice | solution.py:77
  257.0 0.3 squeeze.38
  257.4 1.2 gather_fusion.5
  258.6 0.3 squeeze.37
  258.9 1.2 gather_fusion.4
  260.2 0.3 squeeze.36
  260.5 1.2 gather_fusion.3
  261.8 1.5 select_add_fusion
  263.2 7.3 %all-to-all-start.5 = ((f32[64,2,1152]{2,1,0:T(2,128)}), f32[64,2,1152]{2,1,0:T(2,128)S(1)}, u32[]{:S(2)}, u32[]{:S(2)}) async-start(f32[64,2,1152]{2,1,0:T(2,128)} %select_add_fusion), calls=%async_computation.5 | async-start | bytes 1179648 | tf_op jit(solution)/shard_map/all_to_all | solution.py:80
  270.6 0.2 fusion.64
  270.9 0.1 copy.28
  271.0 0.1 copy.29
  271.1 0.8 fusion.21
  271.8 7.6 %fusion.62 = f32[3]{0:T(128)S(1)} fusion(f32[1]{0:T(128)} %bitcast.15, f32[1]{0:T(128)} %bitcast.14, f32[1]{0:T(128)} %bitcast.13, f32[1]{0:T(128)} %bitcast.19, f32[1]{0:T(128)} %bitcast.17, f32[1]{0:T(128)} %bitcast.16, f32[1]{0:T(128)} %bitcast.23, f32[1]{0:T(128)} %bitcast.21, f32[1]{0:T(128)} %bitcast.20, f32[1]{0:T(128)} %bitcast.27, f32[1]{0:T(128)} %bitcast.25, ...), kind=kLoop, calls=%fused_computation.120 | loop fusion | flops 33 | bytes 60 | tf_op jit(solution)/shard_map/add | solution.py:71
  279.5 0.3 fusion.59
  279.8 107.9 %psum.7 = f32[3]{0:T(128)S(1)} all-reduce(f32[3]{0:T(128)S(1)} %fusion.62), channel_id=1, replica_groups=mesh['dp'=64,'blk'=8] {'dp','blk'}, use_global_device_ids=true, to_apply=%region_12.15 | all-reduce | flops 3 | bytes 24 | tf_op jit(solution)/shard_map/psum | solution.py:84
  387.7 0.5 broadcast_multiply_fusion.1
  388.2 0.2 convolution_add_fusion.2
  388.4 0.2 convolution_add_fusion.1
  388.7 1.1 fusion.1
  389.7 0.4 all_to_all.29
  390.1 1.1 fusion
  (27 shorter events, 0.1 us)
Async XLA Ops:
  0.6 22.6 %copy-start.9 = (s32[3,64]{1,0:T(4,128)S(1)}, s32[3,64]{1,0:T(4,128)}, u32[]{:S(2)}) copy-start(s32[3,64]{1,0:T(4,128)} %param.11) | copy-start | bytes 2308
  6.0 37.8 %all-to-all-start = ((bf16[64,2,1152]{2,1,0:T(2,128)(2,1)}), bf16[64,2,1152]{2,1,0:T(2,128)(2,1)S(1)}, u32[]{:S(2)}, u32[]{:S(2)}) async-start(bf16[64,2,1152]{2,1,0:T(2,128)(2,1)} %reshape.142), calls=%async_computation | async-start | bytes 589824 | tf_op jit(solution)/shard_map/all_to_all | solution.py:56
  50.8 27.5 %all-to-all-start.1 = ((bf16[64,2,1152]{2,1,0:T(2,128)(2,1)}), bf16[64,2,1152]{2,1,0:T(2,128)(2,1)S(1)}, u32[]{:S(2)}, u32[]{:S(2)}) async-start(bf16[64,2,1152]{2,1,0:T(2,128)(2,1)} %reshape.144), calls=%async_computation.1 | async-start | bytes 589824 | tf_op jit(solution)/shard_map/all_to_all | solution.py:59
  64.4 48.5 %copy-start.7 = (f32[128,1152]{1,0:T(8,128)S(1)}, f32[128,1152]{1,0:T(8,128)}, u32[]{:S(2)}) copy-start(f32[128,1152]{1,0:T(8,128)} %param.8) | copy-start | bytes 1769476
  78.4 27.5 %all-to-all-start.2 = ((bf16[64,2,1152]{2,1,0:T(2,128)(2,1)}), bf16[64,2,1152]{2,1,0:T(2,128)(2,1)S(1)}, u32[]{:S(2)}, u32[]{:S(2)}) async-start(bf16[64,2,1152]{2,1,0:T(2,128)(2,1)} %reshape.146), calls=%async_computation.2 | async-start | bytes 589824 | tf_op jit(solution)/shard_map/all_to_all | solution.py:59
  105.9 27.5 %all-to-all-start.3 = ((bf16[64,2,1152]{2,1,0:T(2,128)(2,1)}), bf16[64,2,1152]{2,1,0:T(2,128)(2,1)S(1)}, u32[]{:S(2)}, u32[]{:S(2)}) async-start(bf16[64,2,1152]{2,1,0:T(2,128)(2,1)} %reshape.148), calls=%async_computation.3 | async-start | bytes 589824 | tf_op jit(solution)/shard_map/all_to_all | solution.py:59
  113.2 20.5 %copy-start.3 = (bf16[128,1,1152]{2,1,0:T(2,128)(2,1)}, bf16[128,1,1152]{2,1,0:T(2,128)(2,1)S(1)}, u32[]{:S(2)}) copy-start(bf16[128,1,1152]{2,1,0:T(2,128)(2,1)S(1)} %reshape.145) | copy-start | bytes 884740
  113.5 21.2 %copy-start.1 = (bf16[128,1,1152]{2,1,0:T(2,128)(2,1)}, bf16[128,1,1152]{2,1,0:T(2,128)(2,1)S(1)}, u32[]{:S(2)}) copy-start(bf16[128,1,1152]{2,1,0:T(2,128)(2,1)S(1)} %reshape.147) | copy-start | bytes 884740
  133.7 1.9 copy-start.5
  261.7 8.9 %copy-start = (f32[128,1152]{1,0:T(8,128)S(1)}, f32[128,1152]{1,0:T(8,128)}, u32[]{:S(2)}) copy-start(f32[128,1152]{1,0:T(8,128)} %param.9) | copy-start | bytes 1769476
  263.2 7.8 %copy-start.8 = (s32[128]{0:T(128)S(1)}, s32[128]{0:T(128)}, u32[]{:S(2)}) copy-start(s32[128]{0:T(128)} %param.10) | copy-start | bytes 1540
  263.2 124.9 %copy-start.4 = (bf16[128,1,1152]{2,1,0:T(2,128)(2,1)S(1)}, bf16[128,1,1152]{2,1,0:T(2,128)(2,1)}, u32[]{:S(2)}) copy-start(bf16[128,1,1152]{2,1,0:T(2,128)(2,1)} %copy-done.3) | copy-start | bytes 884740
  263.2 126.5 %all-to-all-start.5 = ((f32[64,2,1152]{2,1,0:T(2,128)}), f32[64,2,1152]{2,1,0:T(2,128)S(1)}, u32[]{:S(2)}, u32[]{:S(2)}) async-start(f32[64,2,1152]{2,1,0:T(2,128)} %select_add_fusion), calls=%async_computation.5 | async-start | bytes 1179648 | tf_op jit(solution)/shard_map/all_to_all | solution.py:80
  270.9 117.6 %copy-start.2 = (bf16[128,1,1152]{2,1,0:T(2,128)(2,1)S(1)}, bf16[128,1,1152]{2,1,0:T(2,128)(2,1)}, u32[]{:S(2)}) copy-start(bf16[128,1,1152]{2,1,0:T(2,128)(2,1)} %copy-done.1) | copy-start | bytes 884740
  279.8 108.9 %copy-start.6 = (bf16[128,1,1152]{2,1,0:T(2,128)(2,1)S(1)}, bf16[128,1,1152]{2,1,0:T(2,128)(2,1)}, u32[]{:S(2)}) copy-start(bf16[128,1,1152]{2,1,0:T(2,128)(2,1)} %copy-done.5) | copy-start | bytes 884740
where the time goes:
time: 392 us; the launch traced here: 391 us
  blocking collectives  223 us (57%)
  waiting for transfers between devices  69.5 us (18%)
  starting transfers between devices  45.5 us (12%)
  local copies, waits for them, and re-layouts  22.5 us (6%)
  other arithmetic  22.3 us (6%)
  matrix products  6.92 us (2%)
    all_to_all x1, blocking collectives, body(): lax.all_to_all(jnp.stack(returned), 'dp', split_axis=1, concat_axis=1, ti...  116 us
    psum x1, blocking collectives, body(): totals = lax.psum(stats, ('dp', 'blk')) / pairs  108 us
    all_to_all x3, waiting for transfers between devices, body(): lax.all_to_all(jnp.take(reorder_slots, plan[step], axis=1).reshape(count,...  49 us
    all_to_all x3, starting transfers between devices, body(): lax.all_to_all(jnp.take(reorder_slots, plan[step], axis=1).reshape(count,...  20.9 us
    all_to_all x1, waiting for transfers between devices, body(): lax.all_to_all(packed, 'dp', split_axis=1, concat_axis=1, tiled=True)  20.5 us
    all_to_all x1, starting transfers between devices, body(): lax.all_to_all(packed, 'dp', split_axis=1, concat_axis=1, tiled=True)  17.2 us
    unnamed x4, other arithmetic  9.59 us
  transfers between devices with their start and end apart: 5, of which 4 were waited for; matrix products, arithmetic and copies ran while one was open for 6% of the time, Pallas kernels for 0%

commit v1 on v0

v1 whole, which is shorter than its diff:
```python
import functools
import math

import jax
import jax.numpy as jnp
from jax import lax
from jax.experimental import pallas as pl
from jax.experimental.pallas import tpu as pltpu
from jax.sharding import PartitionSpec as P

MESH = pl.DeviceIdType.MESH
LOGIT_SHARPNESS = 2.0
LOGIT_OFFSET = -2.0

ROUNDS = 3
CHIPS = 32
PIECES = 16
CHUNKS = 3


def terms(s):
    logit = LOGIT_SHARPNESS * s + LOGIT_OFFSET
    e = jnp.exp(-jnp.abs(logit))
    weight = jnp.where(logit >= 0.0, 1.0, e) / (1.0 + e)
    loss = jnp.maximum(logit, 0.0) + jnp.log1p(e)
    return logit, weight, loss


def nt(a, b):
    return lax.dot_general(a, b, (((1,), (1,)), ((), ())), preferred_element_type=jnp.float32)


def nn(a, b):
    return jnp.dot(a, b, preferred_element_type=jnp.float32)


def wait_bytes(ref, sem):
    pltpu.make_async_copy(ref, ref, sem).wait()


def kernel(
    pairs,
    images, texts, pos_col, pos_row, plan,
    image_grad, text_grad, totals,
    own, rr0, rr1, rr2, stg, arr, stat, red1, red2,
    send1, recv1, sends, recvs, send2, recv2, sendr, recvr,
):
    rr = (rr0, rr1, rr2)
    rows, width = images.shape
    cw = width // CHUNKS
    half_pieces = PIECES // 2
    scale = 1.0 / math.sqrt(width)
    factor = LOGIT_SHARPNESS * scale

    dp = lax.axis_index("dp")
    blk = lax.axis_index("blk")
    core = lax.rem(dp, 2)
    chip = dp // 2
    y, z = chip // 8, lax.rem(chip, 8)
    half = z // 4
    place = y * 4 + lax.rem(z, 4)

    def peer_chip(i):
        return chip ^ i

    def piece_of(t):
        return (t // 8) * 4 + lax.rem(t, 4)

    def mask_in_half(m):
        return (m // 4) * 8 + lax.rem(m, 4)

    def other(i):
        return dp ^ (i // 8), blk ^ lax.rem(i, 8)

    barrier = pltpu.get_barrier_semaphore()

    def greet(i, carry):
        pl.semaphore_signal(barrier, inc=1, device_id=(2 * peer_chip(i) + core, blk), device_id_type=MESH)
        return carry

    lax.fori_loop(1, CHIPS, greet, 0)

    def greet_other(i, carry):
        pl.semaphore_signal(barrier, inc=1, device_id=other(i), device_id_type=MESH)
        return carry

    lax.fori_loop(1, 16, greet_other, 0)

    for c in range(CHUNKS):
        for j in range(half_pieces):
            at = (slice(16 * j, 16 * j + 16), slice(c * cw, (c + 1) * cw))
            own[c, j] = images[at].astype(jnp.bfloat16)
            own[c, half_pieces + j] = texts[at].astype(jnp.bfloat16)
    for c in range(CHUNKS):
        rr[c][core, chip] = own[c, place]

    pl.semaphore_wait(barrier, CHIPS - 1 + 15)

    for c in range(CHUNKS):

        def spread(i, carry, c=c):
            t = peer_chip(i)
            pltpu.make_async_remote_copy(
                src_ref=own.at[c, piece_of(t)],
                dst_ref=rr[c].at[core, chip],
                send_sem=send1.at[c],
                recv_sem=recv1.at[c],
                device_id=(2 * t + core, blk),
                device_id_type=MESH,
            ).start()
            return carry

        lax.fori_loop(1, CHIPS, spread, 0)

    def x_own(c):
        return own[c, :half_pieces].reshape(rows, cw)

    def y_own(c):
        return own[c, half_pieces:].reshape(rows, cw)

    def x_their(c, r):
        return arr[c, :half_pieces, r].reshape(rows, cw)

    def y_their(c, r):
        return arr[c, half_pieces:, r].reshape(rows, cw)

    s = jnp.zeros((rows, rows), jnp.float32)
    st = jnp.zeros((rows, rows), jnp.float32)
    for c in range(CHUNKS):
        s = s + nt(x_own(c), y_own(c))
        st = st + nt(y_own(c), x_own(c))
    s = s * scale
    label = (lax.broadcasted_iota(jnp.int32, (rows, rows), 1) == pos_col[...]).astype(jnp.float32)
    label_t = (lax.broadcasted_iota(jnp.int32, (rows, rows), 0) == pos_row[...]).astype(jnp.float32)
    logit, weight, loss = terms(s)
    weight = weight - label
    loss_sum = loss - label * logit
    weight_sum = weight
    product_sum = weight * s
    weight_b = weight.astype(jnp.bfloat16)
    weight_t = (terms(st * scale)[1] - label_t).astype(jnp.bfloat16)
    for c in range(CHUNKS):
        at = slice(c * cw, (c + 1) * cw)
        image_grad[:, at] = nn(weight_b, y_own(c))
        text_grad[:, at] = nn(weight_t, x_own(c))

    for c in range(CHUNKS):
        wait_bytes(rr[c].at[0, pl.ds(0, CHIPS - 1)], recv1.at[c])
        share = pltpu.make_async_remote_copy(
            src_ref=rr[c].at[core],
            dst_ref=rr[c].at[core],
            send_sem=sends.at[c],
            recv_sem=recvs.at[c],
            device_id=(dp ^ 1, blk),
            device_id_type=MESH,
        )
        share.start()
        share.wait_recv()

        for r in range(ROUNDS):
            p = plan[r, dp]
            arr[c, place, r] = rr[c][lax.rem(p, 2), p // 2]

        def deliver(m, carry, c=c):
            t = peer_chip(mask_in_half(m))
            for r in range(ROUNDS):
                p = plan[r, 2 * t + core]
                stg[c, m, r] = rr[c][lax.rem(p, 2), p // 2]
            pltpu.make_async_remote_copy(
                src_ref=stg.at[c, m],
                dst_ref=arr.at[c, place],
                send_sem=send2.at[c],
                recv_sem=recv2.at[c],
                device_id=(2 * t + core, blk),
                device_id_type=MESH,
            ).start()
            return carry

        lax.fori_loop(1, PIECES, deliver, 0)

    ours = [jnp.zeros((rows, rows), jnp.float32) for _ in range(ROUNDS)]
    theirs = [jnp.zeros((rows, rows), jnp.float32) for _ in range(ROUNDS)]
    for c in range(CHUNKS):
        wait_bytes(arr.at[c, pl.ds(0, PIECES - 1)], recv2.at[c])
        for r in range(ROUNDS):
            ours[r] = ours[r] + nt(x_own(c), y_their(c, r))
            theirs[r] = theirs[r] + nt(y_own(c), x_their(c, r))
    forward, mirrored = [], []
    for r in range(ROUNDS):
        s = ours[r] * scale
        logit, weight, loss = terms(s)
        loss_sum = loss_sum + loss
        weight_sum = weight_sum + weight
        product_sum = product_sum + weight * s
        forward.append(weight.astype(jnp.bfloat16))
    rows_of = [jnp.sum(v, axis=0, keepdims=True) for v in (loss_sum, weight_sum, product_sum)]
    stat[...] = jnp.concatenate(rows_of + [jnp.zeros((5, rows), jnp.float32)], axis=0)

    def reduce_dp(i, carry):
        pltpu.make_async_remote_copy(
            src_ref=stat,
            dst_ref=red1.at[chip],
            send_sem=sendr.at[0],
            recv_sem=recvr.at[0],
            device_id=(2 * peer_chip(i) + core, blk),
            device_id_type=MESH,
        ).start()
        return carry

    lax.fori_loop(1, CHIPS, reduce_dp, 0)
    red1[chip] = stat[...]

    for r in range(ROUNDS):
        mirrored.append(terms(theirs[r] * scale)[1].astype(jnp.bfloat16))
    wait_bytes(red1.at[pl.ds(0, CHIPS - 1)], recvr.at[0])
    mine = 8 * core + blk
    red2[mine] = jnp.sum(red1[...], axis=0)

    def reduce_rest(i, carry):
        pltpu.make_async_remote_copy(
            src_ref=red2.at[mine],
            dst_ref=red2.at[mine],
            send_sem=sendr.at[1],
            recv_sem=recvr.at[1],
            device_id=other(i),
            device_id_type=MESH,
        ).start()
        return carry

    lax.fori_loop(1, 16, reduce_rest, 0)

    for c in range(CHUNKS):
        at = slice(c * cw, (c + 1) * cw)
        image_sum, text_sum = image_grad[:, at], text_grad[:, at]
        for r in range(ROUNDS):
            image_sum = image_sum + nn(forward[r], y_their(c, r))
            text_sum = text_sum + nn(mirrored[r], x_their(c, r))
        image_grad[:, at] = image_sum * factor
        text_grad[:, at] = text_sum * factor

    wait_bytes(red2.at[pl.ds(0, 15)], recvr.at[1])
    total = jnp.sum(red2[...], axis=0)
    for k in range(3):
        totals[k] = jnp.sum(total[k : k + 1, :]) / pairs

    for c in range(CHUNKS):
        wait_bytes(rr[c].at[0, pl.ds(0, CHIPS - 1)], send1.at[c])
        wait_bytes(rr[c].at[0], sends.at[c])
        wait_bytes(arr.at[c, pl.ds(0, PIECES - 1)], send2.at[c])
    wait_bytes(red1.at[pl.ds(0, CHIPS - 1)], sendr.at[0])
    wait_bytes(red2.at[pl.ds(0, 15)], sendr.at[1])


def body(images, texts, positives, plan):
    rows, width = images.shape
    rounds = plan.shape[0]
    pairs = float(rows * rows * (rounds + 1) * lax.axis_size("dp") * lax.axis_size("blk"))
    cw = width // CHUNKS
    vmem = pl.BlockSpec(memory_space=pltpu.VMEM)
    smem = pl.BlockSpec(memory_space=pltpu.SMEM)
    dma = pltpu.SemaphoreType.DMA
    return pl.pallas_call(
        functools.partial(kernel, pairs),
        out_shape=(
            jax.ShapeDtypeStruct((rows, width), jnp.float32),
            jax.ShapeDtypeStruct((rows, width), jnp.float32),
            jax.ShapeDtypeStruct((3,), jnp.float32),
        ),
        in_specs=[vmem, vmem, vmem, vmem, smem],
        out_specs=(vmem, vmem, smem),
        scratch_shapes=[
            pltpu.VMEM((CHUNKS, PIECES, 16, cw), jnp.bfloat16),
            *[pltpu.VMEM((2, CHIPS, 16, cw), jnp.bfloat16) for _ in range(CHUNKS)],
            pltpu.VMEM((CHUNKS, PIECES, ROUNDS, 16, cw), jnp.bfloat16),
            pltpu.VMEM((CHUNKS, PIECES, ROUNDS, 16, cw), jnp.bfloat16),
            pltpu.VMEM((8, rows), jnp.float32),
            pltpu.VMEM((CHIPS, 8, rows), jnp.float32),
            pltpu.VMEM((16, 8, rows), jnp.float32),
            dma((CHUNKS,)), dma((CHUNKS,)),
            dma((CHUNKS,)), dma((CHUNKS,)),
            dma((CHUNKS,)), dma((CHUNKS,)),
            dma((2,)), dma((2,)),
        ],
        compiler_params=pltpu.CompilerParams(
            collective_id=0, has_side_effects=True, vmem_limit_bytes=32 * 1024 * 1024
        ),
        cost_estimate=pl.CostEstimate(flops=600_000_000, bytes_accessed=3_000_000, transcendentals=400_000),
    )(images, texts, positives.reshape(rows, 1), positives.reshape(1, rows), plan)


def solution(mesh):
    placed = (P(("dp", "blk"), None), P(("dp", "blk"), None), P(("dp", "blk")), P())
    return jax.shard_map(
        body,
        mesh=mesh,
        in_specs=placed,
        out_specs=(P(("dp", "blk"), None), P(("dp", "blk"), None), P()),
        check_vma=False,
    )
```

time: 392 us -> 130 us (0.33)
  blocking collectives: 223 us -> 0 us
  Pallas kernels: 0 us -> 123 us
  waiting for transfers between devices: 69.5 us -> 0 us
  starting transfers between devices: 45.5 us -> 0 us
  other arithmetic: 22.3 us -> 0 us
  local copies, waits for them, and re-layouts: 22.5 us -> 5.6 us
  matrix products: 6.92 us -> 0 us
    pallas_call x0 -> x1, Pallas kernels: none -> 123 us  [body(): pl.pallas_call(functools.partial(kernel, pairs), out_shape=(jax.ShapeDtyp...]
    all_to_all x1 -> x0, blocking collectives: 116 us -> none  [body(): lax.all_to_all(jnp.stack(returned), 'dp', split_axis=1, concat_axis=1, ti...]
    psum x1 -> x0, blocking collectives: 108 us -> none  [body(): totals = lax.psum(stats, ('dp', 'blk')) / pairs]
    all_to_all x5 -> x0, waiting for transfers between devices: 69.5 us -> none  [the longest x3 49 us: body(): lax.all_to_all(jnp.take(reorder_slots, plan[step], axis=1).reshape(count,...]
    all_to_all x5 -> x0, starting transfers between devices: 45.5 us -> none  [the longest x3 20.9 us: body(): lax.all_to_all(jnp.take(reorder_slots, plan[step], axis=1).reshape(count,...]
    unnamed x4 -> x0, other arithmetic: 9.59 us -> none
    add x2 -> x0, other arithmetic: 9.11 us -> none  [the longest x1 7.63 us: body(): stats = stats + extra]
    gather x6 -> x0, local copies, waits for them, and re-layouts: 7.23 us -> none  [the longest x3 3.57 us: body(): jnp.take(reorder_slots, plan[step], axis=1).reshape(count, rows, width)]
  transfers between devices with their start and end apart: 5 -> 0, of which waited for: 4 -> 0; matrix products, arithmetic and copies ran while one was open for 6% -> 0% of each run, Pallas kernels for 0% -> 0%
where the time goes in v1:
time: 130 us
  Pallas kernels  123 us (95%)
  local copies, waits for them, and re-layouts  5.6 us (4%)
    pallas_call x1, Pallas kernels, body(): pl.pallas_call(functools.partial(kernel, pairs), out_shape=(jax.ShapeDtyp...  123 us
    unnamed x11, local copies, waits for them, and re-layouts  5.49 us

profile of v1, /device:TPU:1, one launch (start us, length us, event | category | flops | bytes accessed | tf_op | source)
XLA Modules:
  0.0 129.7 jit_solution(12832599968202863814)
XLA Ops:
  0.6 0.0 copy-start
  0.6 0.6 copy-done
  1.3 0.0 copy-start.3
  1.3 0.1 copy.7.pos_col
  1.4 0.6 copy-done.3
  2.0 0.0 copy-start.1
  2.0 1.1 copy-done.1
  3.0 0.0 copy-start.2
  3.0 1.1 copy-done.2
  4.1 123.5 %shard_map.67 = (f32[128,1152]{1,0:T(8,128)S(1)}, f32[128,1152]{1,0:T(8,128)S(1)}, f32[3]{0:T(128)S(1)}) custom-call(f32[128,1152]{1,0:T(8,128)S(1)} %copy-done.1, f32[128,1152]{1,0:T(8,128)S(1)} %copy-done.2, s32[128,1]{1,0:T(8,128)S(1)} %copy.7.pos_col, s32[1,128]{1,0:T(1,128)S(1)} %bitcast.3, s32[3,64]{1,0:T(4,128)S(1)} %copy-done.3), custom_call_target="tpu_custom_call" | custom-call | flops 600000000 | bytes 3000000 | tf_op jit(solution)/shard_map/pallas_call | solution.py:262
  127.6 0.8 copy.11
  128.4 0.8 copy.12
  129.2 0.5 copy.13
Async XLA Ops:
  0.6 0.7 copy-start
  1.3 0.7 copy-start.3
  2.0 1.1 copy-start.1
  3.0 1.1 copy-start.2

commit v2 on v1

v2 whole, which is shorter than its diff:
```python
import functools
import math

import jax
import jax.numpy as jnp
from jax import lax
from jax.experimental import pallas as pl
from jax.experimental.pallas import tpu as pltpu
from jax.sharding import PartitionSpec as P

MESH = pl.DeviceIdType.MESH
LOGIT_SHARPNESS = 2.0
LOGIT_OFFSET = -2.0

ROUNDS = 3
CHIPS = 32
PIECES = 16
LANES = 128
CHUNKS = 9
GROUPS = [("y", g) for g in range(9)] + [("x", g) for g in range(9)]


def terms(s):
    logit = LOGIT_SHARPNESS * s + LOGIT_OFFSET
    e = jnp.exp(-jnp.abs(logit))
    weight = jnp.where(logit >= 0.0, 1.0, e) / (1.0 + e)
    loss = jnp.maximum(logit, 0.0) + jnp.log1p(e)
    return logit, weight, loss


def nt(a, b):
    return lax.dot_general(a, b, (((1,), (1,)), ((), ())), preferred_element_type=jnp.float32)


def nn(a, b):
    return jnp.dot(a, b, preferred_element_type=jnp.float32)


def wait_bytes(ref, sem):
    pltpu.make_async_copy(ref, ref, sem).wait()


def kernel(pairs, images_hbm, texts_hbm, positives_hbm, plan_hbm, image_grad, text_grad, totals, *scratch):
    own, rr, stg, arr = (scratch[k * CHUNKS : (k + 1) * CHUNKS] for k in range(4))
    (
        images, texts, pos_row, plan, xb, yb, stat, red1, red2,
        load, send1, recv1, sends, recvs, send2, recv2, sendr, recvr,
    ) = scratch[4 * CHUNKS :]
    rows, width = images.shape
    row_groups = rows // 16
    scale = 1.0 / math.sqrt(width)
    factor = LOGIT_SHARPNESS * scale

    dp = lax.axis_index("dp")
    blk = lax.axis_index("blk")
    core = lax.rem(dp, 2)
    chip = dp // 2
    place = (chip // 8) * 4 + lax.rem(chip, 4)

    def piece_of(t):
        return (t // 8) * 4 + lax.rem(t, 4)

    def peer_in_half(m):
        return chip ^ ((m // 4) * 8 + lax.rem(m, 4))

    def other(i):
        return dp ^ (i // 8), blk ^ lax.rem(i, 8)

    loads = [
        pltpu.make_async_copy(source, target, load.at[k])
        for k, (source, target) in enumerate(
            [(texts_hbm, texts), (images_hbm, images), (plan_hbm, plan), (positives_hbm, pos_row)]
        )
    ]
    for copy in loads:
        copy.start()

    barrier = pltpu.get_barrier_semaphore()

    def greet(i, carry):
        pl.semaphore_signal(barrier, inc=1, device_id=(2 * (chip ^ i) + core, blk), device_id_type=MESH)
        return carry

    lax.fori_loop(1, CHIPS, greet, 0)

    def greet_other(i, carry):
        pl.semaphore_signal(barrier, inc=1, device_id=other(i), device_id_type=MESH)
        return carry

    lax.fori_loop(1, 16, greet_other, 0)

    loads[0].wait()
    yb[...] = texts[...].astype(jnp.bfloat16)
    loads[1].wait()
    xb[...] = images[...].astype(jnp.bfloat16)
    for position, (kind, g) in enumerate(GROUPS):
        source = yb if kind == "y" else xb
        c, side = position // 2, position % 2
        columns = source[:, g * LANES : (g + 1) * LANES]
        own[c][side * row_groups : (side + 1) * row_groups] = columns.reshape(row_groups, 16, LANES)
    for c in range(CHUNKS):
        rr[c][core, chip] = own[c][place]

    pl.semaphore_wait(barrier, CHIPS - 1 + 15)

    for c in range(CHUNKS):

        def spread(i, carry, c=c):
            t = chip ^ i
            pltpu.make_async_remote_copy(
                src_ref=own[c].at[piece_of(t)],
                dst_ref=rr[c].at[core, chip],
                send_sem=send1.at[c],
                recv_sem=recv1.at[c],
                device_id=(2 * t + core, blk),
                device_id_type=MESH,
            ).start()
            return carry

        lax.fori_loop(1, CHIPS, spread, 0)

    loads[3].wait()
    s = nt(xb[...], yb[...]) * scale
    label_t = (lax.broadcasted_iota(jnp.int32, (rows, rows), 0) == pos_row[...]).astype(jnp.float32)
    label = label_t.T
    logit, weight, loss = terms(s)
    weight = weight - label
    loss_sum = loss - label * logit
    weight_sum = weight
    product_sum = weight * s
    image_grad[...] = nn(weight.astype(jnp.bfloat16), yb[...])
    weight = terms(nt(yb[...], xb[...]) * scale)[1] - label_t
    text_grad[...] = nn(weight.astype(jnp.bfloat16), xb[...])

    loads[2].wait()
    for c in range(CHUNKS):
        wait_bytes(rr[c].at[0, pl.ds(0, CHIPS - 1)], recv1.at[c])
        share = pltpu.make_async_remote_copy(
            src_ref=rr[c].at[core],
            dst_ref=rr[c].at[core],
            send_sem=sends.at[c],
            recv_sem=recvs.at[c],
            device_id=(dp ^ 1, blk),
            device_id_type=MESH,
        )
        share.start()
        share.wait_recv()

        for r in range(ROUNDS):
            p = plan[r, dp]
            arr[c][place, r] = rr[c][lax.rem(p, 2), p // 2]

        def deliver(m, carry, c=c):
            t = peer_in_half(m)
            for r in range(ROUNDS):
                p = plan[r, 2 * t + core]
                stg[c][m, r] = rr[c][lax.rem(p, 2), p // 2]
            pltpu.make_async_remote_copy(
                src_ref=stg[c].at[m],
                dst_ref=arr[c].at[place],
                send_sem=send2.at[c],
                recv_sem=recv2.at[c],
                device_id=(2 * t + core, blk),
                device_id_type=MESH,
            ).start()
            return carry

        lax.fori_loop(1, PIECES, deliver, 0)

    def their(kind, g, r):
        position = GROUPS.index((kind, g))
        c, side = position // 2, position % 2
        return arr[c][side * row_groups : (side + 1) * row_groups, r].reshape(rows, LANES)

    def scores(kind, mine, waited):
        sums = [jnp.zeros((rows, rows), jnp.float32) for _ in range(ROUNDS)]
        for g in range(width // LANES):
            c = GROUPS.index((kind, g)) // 2
            if c not in waited:
                wait_bytes(arr[c].at[pl.ds(0, PIECES - 1)], recv2.at[c])
                waited.add(c)
            for r in range(ROUNDS):
                sums[r] = sums[r] + nt(mine[:, g * LANES : (g + 1) * LANES], their(kind, g, r))
        return sums

    waited = set()
    weights = []
    for s in scores("y", xb, waited):
        s = s * scale
        logit, weight, loss = terms(s)
        loss_sum = loss_sum + loss
        weight_sum = weight_sum + weight
        product_sum = product_sum + weight * s
        weights.append(weight.astype(jnp.bfloat16))
    sums = [jnp.sum(v, axis=0, keepdims=True) for v in (loss_sum, weight_sum, product_sum)]
    stat[...] = jnp.concatenate(sums + [jnp.zeros((5, rows), jnp.float32)], axis=0)

    def reduce_dp(i, carry):
        pltpu.make_async_remote_copy(
            src_ref=stat,
            dst_ref=red1.at[chip],
            send_sem=sendr.at[0],
            recv_sem=recvr.at[0],
            device_id=(2 * (chip ^ i) + core, blk),
            device_id_type=MESH,
        ).start()
        return carry

    lax.fori_loop(1, CHIPS, reduce_dp, 0)
    red1[chip] = stat[...]

    for g in range(width // LANES):
        at = slice(g * LANES, (g + 1) * LANES)
        image_sum = image_grad[:, at]
        for r in range(ROUNDS):
            image_sum = image_sum + nn(weights[r], their("y", g, r))
        image_grad[:, at] = image_sum * factor

    wait_bytes(red1.at[pl.ds(0, CHIPS - 1)], recvr.at[0])
    mine = 8 * core + blk
    red2[mine] = jnp.sum(red1[...], axis=0)

    def reduce_rest(i, carry):
        pltpu.make_async_remote_copy(
            src_ref=red2.at[mine],
            dst_ref=red2.at[mine],
            send_sem=sendr.at[1],
            recv_sem=recvr.at[1],
            device_id=other(i),
            device_id_type=MESH,
        ).start()
        return carry

    lax.fori_loop(1, 16, reduce_rest, 0)

    weights = [terms(s * scale)[1].astype(jnp.bfloat16) for s in scores("x", yb, waited)]
    for g in range(width // LANES):
        at = slice(g * LANES, (g + 1) * LANES)
        text_sum = text_grad[:, at]
        for r in range(ROUNDS):
            text_sum = text_sum + nn(weights[r], their("x", g, r))
        text_grad[:, at] = text_sum * factor

    wait_bytes(red2.at[pl.ds(0, 15)], recvr.at[1])
    total = jnp.sum(red2[...], axis=0)
    for k in range(3):
        totals[k] = jnp.sum(total[k : k + 1, :]) / pairs

    for c in range(CHUNKS):
        wait_bytes(rr[c].at[0, pl.ds(0, CHIPS - 1)], send1.at[c])
        wait_bytes(rr[c].at[0], sends.at[c])
        wait_bytes(arr[c].at[pl.ds(0, PIECES - 1)], send2.at[c])
    wait_bytes(red1.at[pl.ds(0, CHIPS - 1)], sendr.at[0])
    wait_bytes(red2.at[pl.ds(0, 15)], sendr.at[1])


def body(images, texts, positives, plan):
    rows, width = images.shape
    rounds = plan.shape[0]
    pairs = float(rows * rows * (rounds + 1) * lax.axis_size("dp") * lax.axis_size("blk"))
    vmem = pl.BlockSpec(memory_space=pltpu.VMEM)
    smem = pl.BlockSpec(memory_space=pltpu.SMEM)
    hbm = pl.BlockSpec(memory_space=pltpu.HBM)
    dma = pltpu.SemaphoreType.DMA
    sixteen, single = jnp.bfloat16, jnp.float32
    return pl.pallas_call(
        functools.partial(kernel, pairs),
        out_shape=(
            jax.ShapeDtypeStruct((rows, width), single),
            jax.ShapeDtypeStruct((rows, width), single),
            jax.ShapeDtypeStruct((3,), single),
        ),
        in_specs=[hbm, hbm, hbm, hbm],
        out_specs=(vmem, vmem, smem),
        scratch_shapes=[
            *[pltpu.VMEM((PIECES, 16, LANES), sixteen)] * CHUNKS,
            *[pltpu.VMEM((2, CHIPS, 16, LANES), sixteen)] * CHUNKS,
            *[pltpu.VMEM((PIECES, ROUNDS, 16, LANES), sixteen)] * CHUNKS,
            *[pltpu.VMEM((PIECES, ROUNDS, 16, LANES), sixteen)] * CHUNKS,
            pltpu.VMEM((rows, width), single),
            pltpu.VMEM((rows, width), single),
            pltpu.VMEM((1, rows), jnp.int32),
            pltpu.SMEM(plan.shape, jnp.int32),
            pltpu.VMEM((rows, width), sixteen),
            pltpu.VMEM((rows, width), sixteen),
            pltpu.VMEM((8, rows), single),
            pltpu.VMEM((CHIPS, 8, rows), single),
            pltpu.VMEM((16, 8, rows), single),
            dma((4,)),
            dma((CHUNKS,)), dma((CHUNKS,)),
            dma((CHUNKS,)), dma((CHUNKS,)),
            dma((CHUNKS,)), dma((CHUNKS,)),
            dma((2,)), dma((2,)),
        ],
        compiler_params=pltpu.CompilerParams(
            collective_id=0, has_side_effects=True, vmem_limit_bytes=32 * 1024 * 1024
        ),
        cost_estimate=pl.CostEstimate(flops=600_000_000, bytes_accessed=3_000_000, transcendentals=400_000),
    )(images, texts, positives.reshape(1, rows), plan)


def solution(mesh):
    placed = (P(("dp", "blk"), None), P(("dp", "blk"), None), P(("dp", "blk")), P())
    return jax.shard_map(
        body,
        mesh=mesh,
        in_specs=placed,
        out_specs=(P(("dp", "blk"), None), P(("dp", "blk"), None), P()),
        check_vma=False,
    )
```

time: 130 us -> 120 us (0.923)
  Pallas kernels: 123 us -> 113 us
    pallas_call x1, Pallas kernels: 123 us -> 113 us  [body(): pl.pallas_call(functools.partial(kernel, pairs), out_shape=(jax.ShapeDtyp...]
where the time goes in v2:
time: 120 us; the launch traced here: 119 us
  Pallas kernels  113 us (94%)
  local copies, waits for them, and re-layouts  5.6 us (5%)
    pallas_call x1, Pallas kernels, body(): pl.pallas_call(functools.partial(kernel, pairs), out_shape=(jax.ShapeDtyp...  113 us
    unnamed x11, local copies, waits for them, and re-layouts  5.6 us

profile of v2, /device:TPU:1, one launch (start us, length us, event | category | flops | bytes accessed | tf_op | source)
XLA Modules:
  0.0 119.3 jit_solution(8263312959756572410)
XLA Ops:
  0.6 0.0 copy-start.3
  0.6 0.6 copy-done.3
  1.3 0.0 copy-start
  1.3 1.1 copy-done
  2.4 0.0 copy-start.1
  2.4 1.1 copy-done.1
  3.4 0.0 copy-start.2
  3.4 0.7 copy-done.2
  4.1 113.1 %shard_map.67 = (f32[128,1152]{1,0:T(8,128)S(1)}, f32[128,1152]{1,0:T(8,128)S(1)}, f32[3]{0:T(128)S(1)}) custom-call(f32[128,1152]{1,0:T(8,128)S(1)} %copy-done, f32[128,1152]{1,0:T(8,128)S(1)} %copy-done.1, s32[1,128]{1,0:T(1,128)S(1)} %bitcast.1, s32[3,64]{1,0:T(4,128)S(1)} %copy-done.2), custom_call_target="tpu_custom_call" | custom-call | flops 600000000 | bytes 3000000 | tf_op jit(solution)/shard_map/pallas_call | solution.py:266
  117.2 0.8 copy.10
  118.0 0.8 copy.11
  118.8 0.5 copy.12
Async XLA Ops:
  0.6 0.7 copy-start.3
  1.3 1.1 copy-start
  2.4 1.1 copy-start.1
  3.4 0.7 copy-start.2

commit v3 on v2

--- a/solution.py
+++ b/solution.py
@@ -17,6 +17,10 @@
 PIECES = 16
 LANES = 128
 CHUNKS = 9
+FLIGHT = 3
+TEXTS_AT = 4
+SECOND_AT = 5
+THIRD_AT = 6
 GROUPS = [("y", g) for g in range(9)] + [("x", g) for g in range(9)]
 
 
@@ -43,7 +47,7 @@
 def kernel(pairs, images_hbm, texts_hbm, positives_hbm, plan_hbm, image_grad, text_grad, totals, *scratch):
     own, rr, stg, arr = (scratch[k * CHUNKS : (k + 1) * CHUNKS] for k in range(4))
     (
-        images, texts, pos_row, plan, xb, yb, stat, red1, red2,
+        images, texts, pos_row, plan, xb, yb, stat, stat_z, stat_core, stat_sibling, red1, red2,
         load, send1, recv1, sends, recvs, send2, recv2, sendr, recvr,
     ) = scratch[4 * CHUNKS :]
     rows, width = images.shape
@@ -63,8 +67,11 @@
     def peer_in_half(m):
         return chip ^ ((m // 4) * 8 + lax.rem(m, 4))
 
-    def other(i):
-        return dp ^ (i // 8), blk ^ lax.rem(i, 8)
+    def along_z(i):
+        return dp ^ (2 * lax.rem(i, 8)), blk ^ (4 * (i // 8))
+
+    def across(i):
+        return dp ^ (16 * (i // 4)), blk ^ lax.rem(i, 4)
 
     loads = [
         pltpu.make_async_copy(source, target, load.at[k])
@@ -83,11 +90,20 @@
 
     lax.fori_loop(1, CHIPS, greet, 0)
 
-    def greet_other(i, carry):
-        pl.semaphore_signal(barrier, inc=1, device_id=other(i), device_id_type=MESH)
+    pl.semaphore_signal(barrier, inc=1, device_id=(dp ^ 1, blk), device_id_type=MESH)
+
+    def greet_z(i, carry):
+        pl.semaphore_signal(barrier, inc=1, device_id=along_z(i), device_id_type=MESH)
         return carry
 
-    lax.fori_loop(1, 16, greet_other, 0)
+    lax.fori_loop(8, 16, greet_z, 0)
+
+    def greet_across(i, carry):
+        other = across((i // 3) * 4 + lax.rem(i, 3) + 1)
+        pl.semaphore_signal(barrier, inc=1, device_id=other, device_id_type=MESH)
+        return carry
+
+    lax.fori_loop(0, 12, greet_across, 0)
 
     loads[0].wait()
     yb[...] = texts[...].astype(jnp.bfloat16)
@@ -101,11 +117,10 @@
     for c in range(CHUNKS):
         rr[c][core, chip] = own[c][place]
 
-    pl.semaphore_wait(barrier, CHIPS - 1 + 15)
-
-    for c in range(CHUNKS):
-
-        def spread(i, carry, c=c):
+    pl.semaphore_wait(barrier, CHIPS + 8 + 12)
+
+    def spread(c):
+        def send(i, carry):
             t = chip ^ i
             pltpu.make_async_remote_copy(
                 src_ref=own[c].at[piece_of(t)],
@@ -117,7 +132,10 @@
             ).start()
             return carry
 
-        lax.fori_loop(1, CHIPS, spread, 0)
+        lax.fori_loop(1, CHIPS, send, 0)
+
+    for c in range(FLIGHT):
+        spread(c)
 
     loads[3].wait()
     s = nt(xb[...], yb[...]) * scale
@@ -132,8 +150,7 @@
     weight = terms(nt(yb[...], xb[...]) * scale)[1] - label_t
     text_grad[...] = nn(weight.astype(jnp.bfloat16), xb[...])
 
-    loads[2].wait()
-    for c in range(CHUNKS):
+    def deliver(c):
         wait_bytes(rr[c].at[0, pl.ds(0, CHIPS - 1)], recv1.at[c])
         share = pltpu.make_async_remote_copy(
             src_ref=rr[c].at[core],
@@ -150,7 +167,7 @@
             p = plan[r, dp]
             arr[c][place, r] = rr[c][lax.rem(p, 2), p // 2]
 
-        def deliver(m, carry, c=c):
+        def send(m, carry):
             t = peer_in_half(m)
             for r in range(ROUNDS):
                 p = plan[r, 2 * t + core]
@@ -165,7 +182,9 @@
             ).start()
             return carry
 
-        lax.fori_loop(1, PIECES, deliver, 0)
+        lax.fori_loop(1, PIECES, send, 0)
+        if c + FLIGHT < CHUNKS:
+            spread(c + FLIGHT)
 
     def their(kind, g, r):
         position = GROUPS.index((kind, g))
@@ -183,6 +202,10 @@
                 sums[r] = sums[r] + nt(mine[:, g * LANES : (g + 1) * LANES], their(kind, g, r))
         return sums
 
+    loads[2].wait()
+    for c in range(TEXTS_AT + 1):
+        deliver(c)
+
     waited = set()
     weights = []
     for s in scores("y", xb, waited):
@@ -192,22 +215,50 @@
         weight_sum = weight_sum + weight
         product_sum = product_sum + weight * s
         weights.append(weight.astype(jnp.bfloat16))
-    sums = [jnp.sum(v, axis=0, keepdims=True) for v in (loss_sum, weight_sum, product_sum)]
-    stat[...] = jnp.concatenate(sums + [jnp.zeros((5, rows), jnp.float32)], axis=0)
-
-    def reduce_dp(i, carry):
-        pltpu.make_async_remote_copy(
-            src_ref=stat,
-            dst_ref=red1.at[chip],
-            send_sem=sendr.at[0],
-            recv_sem=recvr.at[0],
-            device_id=(2 * (chip ^ i) + core, blk),
-            device_id_type=MESH,
-        ).start()
-        return carry
-
-    lax.fori_loop(1, CHIPS, reduce_dp, 0)
-    red1[chip] = stat[...]
+    lane = lax.broadcasted_iota(jnp.int32, (1, rows), 1)
+    stat[...] = jnp.zeros((1, rows), jnp.float32)
+    for k, v in enumerate((loss_sum, weight_sum, product_sum)):
+        stat[...] += jnp.where(lane == k, jnp.sum(v), 0.0)
+
+    def exchange(k, source, slots, at, peer):
+        slots[at] = source[...]
+
+        def send(i, carry):
+            pltpu.make_async_remote_copy(
+                src_ref=source,
+                dst_ref=slots.at[at],
+                send_sem=sendr.at[k],
+                recv_sem=recvr.at[k],
+                device_id=peer(i),
+                device_id_type=MESH,
+            ).start()
+            return carry
+
+        lax.fori_loop(1, 16, send, 0)
+
+    exchange(0, stat, red1, (blk // 4) * 8 + lax.rem(chip, 8), along_z)
+    for c in range(TEXTS_AT + 1, SECOND_AT + 1):
+        deliver(c)
+
+    wait_bytes(red1.at[pl.ds(0, 15)], recvr.at[0])
+    stat_z[...] = jnp.sum(red1[...], axis=0)
+    exchange(1, stat_z, red2, (chip // 8) * 4 + lax.rem(blk, 4), across)
+    for c in range(SECOND_AT + 1, THIRD_AT + 1):
+        deliver(c)
+
+    wait_bytes(red2.at[pl.ds(0, 15)], recvr.at[1])
+    stat_core[...] = jnp.sum(red2[...], axis=0)
+    swap = pltpu.make_async_remote_copy(
+        src_ref=stat_core,
+        dst_ref=stat_sibling,
+        send_sem=sendr.at[2],
+        recv_sem=recvr.at[2],
+        device_id=(dp ^ 1, blk),
+        device_id_type=MESH,
+    )
+    swap.start()
+    for c in range(THIRD_AT + 1, CHUNKS):
+        deliver(c)
 
     for g in range(width // LANES):
         at = slice(g * LANES, (g + 1) * LANES)
@@ -215,23 +266,6 @@
         for r in range(ROUNDS):
             image_sum = image_sum + nn(weights[r], their("y", g, r))
         image_grad[:, at] = image_sum * factor
-
-    wait_bytes(red1.at[pl.ds(0, CHIPS - 1)], recvr.at[0])
-    mine = 8 * core + blk
-    red2[mine] = jnp.sum(red1[...], axis=0)
-
-    def reduce_rest(i, carry):
-        pltpu.make_async_remote_copy(
-            src_ref=red2.at[mine],
-            dst_ref=red2.at[mine],
-            send_sem=sendr.at[1],
-            recv_sem=recvr.at[1],
-            device_id=other(i),
-            device_id_type=MESH,
-        ).start()
-        return carry
-
-    lax.fori_loop(1, 16, reduce_rest, 0)
 
     weights = [terms(s * scale)[1].astype(jnp.bfloat16) for s in scores("x", yb, waited)]
     for g in range(width // LANES):
@@ -241,17 +275,18 @@
             text_sum = text_sum + nn(weights[r], their("x", g, r))
         text_grad[:, at] = text_sum * factor
 
-    wait_bytes(red2.at[pl.ds(0, 15)], recvr.at[1])
-    total = jnp.sum(red2[...], axis=0)
+    swap.wait_recv()
+    total = stat_core[...] + stat_sibling[...]
     for k in range(3):
-        totals[k] = jnp.sum(total[k : k + 1, :]) / pairs
+        totals[k] = jnp.sum(jnp.where(lane == k, total, 0.0)) / pairs
 
     for c in range(CHUNKS):
         wait_bytes(rr[c].at[0, pl.ds(0, CHIPS - 1)], send1.at[c])
         wait_bytes(rr[c].at[0], sends.at[c])
         wait_bytes(arr[c].at[pl.ds(0, PIECES - 1)], send2.at[c])
-    wait_bytes(red1.at[pl.ds(0, CHIPS - 1)], sendr.at[0])
+    wait_bytes(red1.at[pl.ds(0, 15)], sendr.at[0])
     wait_bytes(red2.at[pl.ds(0, 15)], sendr.at[1])
+    swap.wait_send()
 
 
 def body(images, texts, positives, plan):
@@ -283,17 +318,16 @@
             pltpu.SMEM(plan.shape, jnp.int32),
             pltpu.VMEM((rows, width), sixteen),
             pltpu.VMEM((rows, width), sixteen),
-            pltpu.VMEM((8, rows), single),
-            pltpu.VMEM((CHIPS, 8, rows), single),
-            pltpu.VMEM((16, 8, rows), single),
+            *[pltpu.VMEM((1, rows), single)] * 4,
+            *[pltpu.VMEM((16, 1, rows), single)] * 2,
             dma((4,)),
             dma((CHUNKS,)), dma((CHUNKS,)),
             dma((CHUNKS,)), dma((CHUNKS,)),
             dma((CHUNKS,)), dma((CHUNKS,)),
-            dma((2,)), dma((2,)),
+            dma((3,)), dma((3,)),
         ],
         compiler_params=pltpu.CompilerParams(
-            collective_id=0, has_side_effects=True, vmem_limit_bytes=32 * 1024 * 1024
+            collective_id=0, has_side_effects=True, vmem_limit_bytes=53 * 1024 * 1024
         ),
         cost_estimate=pl.CostEstimate(flops=600_000_000, bytes_accessed=3_000_000, transcendentals=400_000),
     )(images, texts, positives.reshape(1, rows), plan)

time: 120 us -> 110 us (0.917)
  Pallas kernels: 113 us -> 104 us
  local copies, waits for them, and re-layouts: 5.6 us -> 3.92 us
    pallas_call x1, Pallas kernels: 113 us -> 104 us  [body(): pl.pallas_call(functools.partial(kernel, pairs), out_shape=(jax.ShapeDtyp...]
    unnamed x11 -> x9, local copies, waits for them, and re-layouts: 5.6 us -> 3.92 us
where the time goes in v3:
time: 110 us; the launch traced here: 109 us
  Pallas kernels  104 us (95%)
  local copies, waits for them, and re-layouts  3.92 us (4%)
    pallas_call x1, Pallas kernels, body(): pl.pallas_call(functools.partial(kernel, pairs), out_shape=(jax.ShapeDtyp...  104 us
    unnamed x9, local copies, waits for them, and re-layouts  3.92 us

profile of v3, /device:TPU:1, one launch (start us, length us, event | category | flops | bytes accessed | tf_op | source)
XLA Modules:
  0.0 109.0 jit_solution(2061450259508067262)
XLA Ops:
  0.6 0.0 copy-start.1
  0.6 0.6 copy-done.1
  1.3 0.0 copy-start
  1.3 0.7 copy-done
  2.0 104.4 %shard_map.67 = (f32[128,1152]{1,0:T(8,128)S(1)}, f32[128,1152]{1,0:T(8,128)}, f32[3]{0:T(128)S(1)}) custom-call(f32[128,1152]{1,0:T(8,128)} %images_hbm.1, f32[128,1152]{1,0:T(8,128)} %texts_hbm.1, s32[1,128]{1,0:T(1,128)S(1)} %bitcast.1, s32[3,64]{1,0:T(4,128)S(1)} %copy-done), custom_call_target="tpu_custom_call" | custom-call | flops 600000000 | bytes 3000000 | tf_op jit(solution)/shard_map/pallas_call | solution.py:301
  106.4 0.0 copy-start.2
  106.4 0.8 copy.10
  107.2 0.5 copy-done.2
  107.7 0.8 copy.11
  108.5 0.5 copy.12
Async XLA Ops:
  0.6 0.7 copy-start.1
  1.3 0.7 copy-start
  106.4 1.3 %copy-start.2 = (f32[128,1152]{1,0:T(8,128)S(1)}, f32[128,1152]{1,0:T(8,128)}, u32[]{:S(2)}) copy-start(f32[128,1152]{1,0:T(8,128)} %get-tuple-element.7) | copy-start | bytes 1769476

commit v4 on v3

--- a/solution.py
+++ b/solution.py
@@ -18,9 +18,10 @@
 LANES = 128
 CHUNKS = 9
 FLIGHT = 3
-TEXTS_AT = 4
-SECOND_AT = 5
-THIRD_AT = 6
+TEXTS_AT = 5
+FIRST_AT = 5
+SECOND_AT = 6
+THIRD_AT = 7
 GROUPS = [("y", g) for g in range(9)] + [("x", g) for g in range(9)]
 
 
@@ -47,8 +48,8 @@
 def kernel(pairs, images_hbm, texts_hbm, positives_hbm, plan_hbm, image_grad, text_grad, totals, *scratch):
     own, rr, stg, arr = (scratch[k * CHUNKS : (k + 1) * CHUNKS] for k in range(4))
     (
-        images, texts, pos_row, plan, xb, yb, stat, stat_z, stat_core, stat_sibling, red1, red2,
-        load, send1, recv1, sends, recvs, send2, recv2, sendr, recvr,
+        images, texts, pos_row, plan, xb, yb, stat, stat_z, stat_all, stat_sibling, red1, red2,
+        load, send1, recv1, sends, recvs, send2, recv2, sendr, recvr, ready,
     ) = scratch[4 * CHUNKS :]
     rows, width = images.shape
     row_groups = rows // 16
@@ -85,25 +86,27 @@
     barrier = pltpu.get_barrier_semaphore()
 
     def greet(i, carry):
-        pl.semaphore_signal(barrier, inc=1, device_id=(2 * (chip ^ i) + core, blk), device_id_type=MESH)
+        pl.semaphore_signal(barrier, inc=1, device_id=(2 * (chip ^ i), blk), device_id_type=MESH)
         return carry
 
     lax.fori_loop(1, CHIPS, greet, 0)
 
-    pl.semaphore_signal(barrier, inc=1, device_id=(dp ^ 1, blk), device_id_type=MESH)
-
-    def greet_z(i, carry):
-        pl.semaphore_signal(barrier, inc=1, device_id=along_z(i), device_id_type=MESH)
-        return carry
-
-    lax.fori_loop(8, 16, greet_z, 0)
-
-    def greet_across(i, carry):
-        other = across((i // 3) * 4 + lax.rem(i, 3) + 1)
-        pl.semaphore_signal(barrier, inc=1, device_id=other, device_id_type=MESH)
-        return carry
-
-    lax.fori_loop(0, 12, greet_across, 0)
+    @pl.when(core == 1)
+    def _():
+        pl.semaphore_signal(barrier, inc=1, device_id=(dp ^ 1, blk), device_id_type=MESH)
+
+        def greet_z(i, carry):
+            pl.semaphore_signal(barrier, inc=1, device_id=along_z(i), device_id_type=MESH)
+            return carry
+
+        lax.fori_loop(8, 16, greet_z, 0)
+
+        def greet_across(i, carry):
+            other = across((i // 3) * 4 + lax.rem(i, 3) + 1)
+            pl.semaphore_signal(barrier, inc=1, device_id=other, device_id_type=MESH)
+            return carry
+
+        lax.fori_loop(0, 12, greet_across, 0)
 
     loads[0].wait()
     yb[...] = texts[...].astype(jnp.bfloat16)
@@ -117,7 +120,14 @@
     for c in range(CHUNKS):
         rr[c][core, chip] = own[c][place]
 
-    pl.semaphore_wait(barrier, CHIPS + 8 + 12)
+    @pl.when(core == 0)
+    def _():
+        pl.semaphore_wait(barrier, 2 * CHIPS - 1)
+        pl.semaphore_signal(ready, inc=1, device_id=(dp ^ 1, blk), device_id_type=MESH)
+
+    @pl.when(core == 1)
+    def _():
+        pl.semaphore_wait(ready, 1)
 
     def spread(c):
         def send(i, carry):
@@ -236,27 +246,49 @@
 
         lax.fori_loop(1, 16, send, 0)
 
-    exchange(0, stat, red1, (blk // 4) * 8 + lax.rem(chip, 8), along_z)
-    for c in range(TEXTS_AT + 1, SECOND_AT + 1):
-        deliver(c)
-
-    wait_bytes(red1.at[pl.ds(0, 15)], recvr.at[0])
-    stat_z[...] = jnp.sum(red1[...], axis=0)
-    exchange(1, stat_z, red2, (chip // 8) * 4 + lax.rem(blk, 4), across)
+    def to_sibling(k, source):
+        return pltpu.make_async_remote_copy(
+            src_ref=source,
+            dst_ref=stat_sibling,
+            send_sem=sendr.at[k],
+            recv_sem=recvr.at[k],
+            device_id=(dp ^ 1, blk),
+            device_id_type=MESH,
+        )
+
+    @pl.when(core == 0)
+    def _():
+        to_sibling(2, stat).start()
+
+    for c in range(TEXTS_AT + 1, FIRST_AT + 1):
+        deliver(c)
+
+    @pl.when(core == 1)
+    def _():
+        to_sibling(2, stat).wait_recv()
+        stat[...] += stat_sibling[...]
+        pl.semaphore_wait(barrier, 8 + 12)
+        exchange(0, stat, red1, (blk // 4) * 8 + lax.rem(chip, 8), along_z)
+
+    for c in range(FIRST_AT + 1, SECOND_AT + 1):
+        deliver(c)
+
+    @pl.when(core == 1)
+    def _():
+        wait_bytes(red1.at[pl.ds(0, 15)], recvr.at[0])
+        stat_z[...] = jnp.sum(red1[...], axis=0)
+        exchange(1, stat_z, red2, (chip // 8) * 4 + lax.rem(blk, 4), across)
+
     for c in range(SECOND_AT + 1, THIRD_AT + 1):
         deliver(c)
 
-    wait_bytes(red2.at[pl.ds(0, 15)], recvr.at[1])
-    stat_core[...] = jnp.sum(red2[...], axis=0)
-    swap = pltpu.make_async_remote_copy(
-        src_ref=stat_core,
-        dst_ref=stat_sibling,
-        send_sem=sendr.at[2],
-        recv_sem=recvr.at[2],
-        device_id=(dp ^ 1, blk),
-        device_id_type=MESH,
-    )
-    swap.start()
+    @pl.when(core == 1)
+    def _():
+        wait_bytes(red2.at[pl.ds(0, 15)], recvr.at[1])
+        stat_all[...] = jnp.sum(red2[...], axis=0)
+        stat_sibling[...] = stat_all[...]
+        to_sibling(3, stat_all).start()
+
     for c in range(THIRD_AT + 1, CHUNKS):
         deliver(c)
 
@@ -275,8 +307,11 @@
             text_sum = text_sum + nn(weights[r], their("x", g, r))
         text_grad[:, at] = text_sum * factor
 
-    swap.wait_recv()
-    total = stat_core[...] + stat_sibling[...]
+    @pl.when(core == 0)
+    def _():
+        to_sibling(3, stat_all).wait_recv()
+
+    total = stat_sibling[...]
     for k in range(3):
         totals[k] = jnp.sum(jnp.where(lane == k, total, 0.0)) / pairs
 
@@ -284,9 +319,16 @@
         wait_bytes(rr[c].at[0, pl.ds(0, CHIPS - 1)], send1.at[c])
         wait_bytes(rr[c].at[0], sends.at[c])
         wait_bytes(arr[c].at[pl.ds(0, PIECES - 1)], send2.at[c])
-    wait_bytes(red1.at[pl.ds(0, 15)], sendr.at[0])
-    wait_bytes(red2.at[pl.ds(0, 15)], sendr.at[1])
-    swap.wait_send()
+
+    @pl.when(core == 0)
+    def _():
+        to_sibling(2, stat).wait_send()
+
+    @pl.when(core == 1)
+    def _():
+        wait_bytes(red1.at[pl.ds(0, 15)], sendr.at[0])
+        wait_bytes(red2.at[pl.ds(0, 15)], sendr.at[1])
+        to_sibling(3, stat_all).wait_send()
 
 
 def body(images, texts, positives, plan):
@@ -324,10 +366,11 @@
             dma((CHUNKS,)), dma((CHUNKS,)),
             dma((CHUNKS,)), dma((CHUNKS,)),
             dma((CHUNKS,)), dma((CHUNKS,)),
-            dma((3,)), dma((3,)),
+            dma((4,)), dma((4,)),
+            pltpu.SemaphoreType.REGULAR,
         ],
         compiler_params=pltpu.CompilerParams(
-            collective_id=0, has_side_effects=True, vmem_limit_bytes=53 * 1024 * 1024
+            collective_id=0, has_side_effects=True, vmem_limit_bytes=60 * 1024 * 1024
         ),
         cost_estimate=pl.CostEstimate(flops=600_000_000, bytes_accessed=3_000_000, transcendentals=400_000),
     )(images, texts, positives.reshape(1, rows), plan)

time: 110 us -> 107 us (0.973)
  Pallas kernels: 104 us -> 102 us
    pallas_call x1, Pallas kernels: 104 us -> 102 us  [body(): pl.pallas_call(functools.partial(kernel, pairs), out_shape=(jax.ShapeDtyp...]
    unnamed x9 -> x7, local copies, waits for them, and re-layouts: 3.92 us -> 3.31 us
where the time goes in v4:
time: 107 us; the launch traced here: 106 us
  Pallas kernels  102 us (95%)
  local copies, waits for them, and re-layouts  3.31 us (3%)
    pallas_call x1, Pallas kernels, body(): pl.pallas_call(functools.partial(kernel, pairs), out_shape=(jax.ShapeDtyp...  102 us
    unnamed x7, local copies, waits for them, and re-layouts  3.31 us

profile of v4, /device:TPU:1, one launch (start us, length us, event | category | flops | bytes accessed | tf_op | source)
XLA Modules:
  0.0 106.0 jit_solution(1570004709228733570)
XLA Ops:
  0.6 102.1 %shard_map.67 = (f32[128,1152]{1,0:T(8,128)}, f32[128,1152]{1,0:T(8,128)}, f32[3]{0:T(128)}) custom-call(f32[128,1152]{1,0:T(8,128)} %images_hbm.1, f32[128,1152]{1,0:T(8,128)} %texts_hbm.1, s32[1,128]{1,0:T(1,128)} %bitcast.1, s32[3,64]{1,0:T(4,128)} %plan_hbm.1), custom_call_target="tpu_custom_call" | custom-call | flops 600000000 | bytes 3000000 | tf_op jit(solution)/shard_map/pallas_call | solution.py:343
  102.7 0.0 copy-start
  102.7 2.0 %copy.10 = f32[128,1152]{1,0:T(8,128)} copy(f32[128,1152]{1,0:T(8,128)} %get-tuple-element.6) | data formatting | bytes 1179648
  104.7 0.0 copy-done
  104.7 0.0 copy-start.1
  104.7 0.8 copy.11
  105.5 0.0 copy-done.1
  105.5 0.5 copy.12
Async XLA Ops:
  102.7 2.0 %copy-start = (f32[128,1152]{1,0:T(8,128)S(1)}, f32[128,1152]{1,0:T(8,128)}, u32[]{:S(2)}) copy-start(f32[128,1152]{1,0:T(8,128)} %get-tuple-element.7) | copy-start | bytes 1769476
  104.7 0.8 copy-start.1

commit v5 on v4

--- a/solution.py
+++ b/solution.py
@@ -20,8 +20,8 @@
 FLIGHT = 3
 TEXTS_AT = 5
 FIRST_AT = 5
-SECOND_AT = 6
-THIRD_AT = 7
+SECOND_AT = 7
+THIRD_AT = 8
 GROUPS = [("y", g) for g in range(9)] + [("x", g) for g in range(9)]
 
 

time: 107 us -> 106 us (level)
  no operation moved by 1% of the time
where the time goes in v5:
time: 106 us
  Pallas kernels  102 us (96%)
  local copies, waits for them, and re-layouts  3.31 us (3%)
    pallas_call x1, Pallas kernels, body(): pl.pallas_call(functools.partial(kernel, pairs), out_shape=(jax.ShapeDtyp...  102 us
    unnamed x7, local copies, waits for them, and re-layouts  3.31 us

profile of v5, /device:TPU:1, one launch (start us, length us, event | category | flops | bytes accessed | tf_op | source)
XLA Modules:
  0.0 105.9 jit_solution(14935094394699371520)
XLA Ops:
  0.6 101.9 %shard_map.67 = (f32[128,1152]{1,0:T(8,128)}, f32[128,1152]{1,0:T(8,128)}, f32[3]{0:T(128)}) custom-call(f32[128,1152]{1,0:T(8,128)} %images_hbm.1, f32[128,1152]{1,0:T(8,128)} %texts_hbm.1, s32[1,128]{1,0:T(1,128)} %bitcast.1, s32[3,64]{1,0:T(4,128)} %plan_hbm.1), custom_call_target="tpu_custom_call" | custom-call | flops 600000000 | bytes 3000000 | tf_op jit(solution)/shard_map/pallas_call | solution.py:343
  102.5 0.0 copy-start
  102.5 2.0 %copy.10 = f32[128,1152]{1,0:T(8,128)} copy(f32[128,1152]{1,0:T(8,128)} %get-tuple-element.6) | data formatting | bytes 1179648
  104.5 0.0 copy-done
  104.5 0.0 copy-start.1
  104.5 0.8 copy.11
  105.3 0.0 copy-done.1
  105.3 0.5 copy.12
Async XLA Ops:
  102.5 2.0 %copy-start = (f32[128,1152]{1,0:T(8,128)S(1)}, f32[128,1152]{1,0:T(8,128)}, u32[]{:S(2)}) copy-start(f32[128,1152]{1,0:T(8,128)} %get-tuple-element.7) | copy-start | bytes 1769476
  104.5 0.8 copy-start.1
